TPU v7x, 512 devices: a whole 4x4x16 slice. The times are simulated.
512 devices in a mesh: dp: 16 (over z), seq: 32 (over x, y, core).
Axes of the slice: x: 4, y: 4, z: 16, core: 2. Of those that a mesh axis runs over, the one named last changes fastest.
Arguments:
- queries: bfloat16 [16, 4096, 2048], P('dp', 'seq'), may hold values from -90 to 90
- keys: bfloat16 [16, 4096, 2048], P('dp', 'seq'), may hold values from -6 to 6
- values: bfloat16 [16, 4096, 2048], P('dp', 'seq'), may hold values from -6 to 6
- d_out: bfloat16 [16, 4096, 2048], P('dp', 'seq'), may hold values from -6 to 6
- cluster_ids: int32 [16, 4096, 16], P('dp', 'seq'), may hold values from 0 to 63, as said below
- gain: float32 [2048], replicated, may hold values from 0.1 to 1.9
Outputs:
- query_grad: bfloat16 [16, 4096, 2048], P('dp', 'seq')
- key_grad: bfloat16 [16, 4096, 2048], P('dp', 'seq')
- value_grad: bfloat16 [16, 4096, 2048], P('dp', 'seq')
- gain_grad: float32 [2048], replicated
Inputs may be any that keep to these rules, and one draw needn't show every extreme that they name: `cluster_ids`: cluster c belongs to owner c // 2. For every sequence and head, the 128 positions held by one seq index name clusters of every owner, exactly 4 positions for each.
All inputs are finite; a program needn't handle non-finite values.
Results may differ from a plain program's by a relative error of at most 0.0067.
Values may be sent and summed in bfloat16 or wider, within the bound.
A program may use at most 64 MiB of HBM per device.

v0:
```python
import jax
import jax.numpy as jnp
from jax import lax
from jax.sharding import PartitionSpec as P

H = 16
HD = 128
CPO = 2


def attend(payload):
    rows_in, labels = payload
    width = rows_in.shape[1] // 4
    query = rows_in[:, :width]
    scaled = rows_in[:, width : 2 * width]
    value = rows_in[:, 2 * width : 3 * width]
    upstream = rows_in[:, 3 * width :]
    factor = HD ** (-0.5)
    scores = jnp.dot(query, scaled.T, preferred_element_type=jnp.float32) * factor
    positions = jnp.arange(query.shape[0])
    allowed = (labels[:, None] == labels[None, :]) & (positions[None, :] <= positions[:, None])
    scores = jnp.where(allowed, scores, -jnp.inf)
    maximum = jnp.max(scores, axis=1, keepdims=True)
    expo = jnp.where(allowed, jnp.exp(scores - maximum), 0.0)
    weights = expo / jnp.sum(expo, axis=1, keepdims=True)
    rounded = weights.astype(jnp.bfloat16)
    output = jnp.dot(rounded, value, preferred_element_type=jnp.float32)
    deltas = jnp.sum(upstream.astype(jnp.float32) * output, axis=1)
    value_grad = jnp.dot(rounded.T, upstream, preferred_element_type=jnp.float32).astype(
        jnp.bfloat16
    )
    inner = jnp.dot(upstream, value.T, preferred_element_type=jnp.float32)
    score_grad = (weights * (inner - deltas[:, None])).astype(jnp.bfloat16)
    query_grad = (jnp.dot(score_grad, scaled, preferred_element_type=jnp.float32) * factor).astype(
        jnp.bfloat16
    )
    scaled_grad = (
        jnp.dot(score_grad.T, query, preferred_element_type=jnp.float32) * factor
    ).astype(jnp.bfloat16)
    return jnp.concatenate([query_grad, scaled_grad, value_grad], axis=1)


def owner_work(arrived):
    rows_in, labels = arrived
    heads_here, sources, depth, width = rows_in.shape
    result = lax.map(
        attend,
        (
            rows_in.reshape(heads_here, sources * depth, width),
            labels.reshape(heads_here, sources * depth),
        ),
    )
    return result.reshape(heads_here, sources, depth, result.shape[-1])


def on_device(queries, keys, values, d_out, cluster_ids, gain):
    count_rows = queries.shape[1]
    owners_count = lax.axis_size("seq")
    per_owner = count_rows // owners_count
    gain_heads = gain.reshape(H, HD)
    scaled_keys = (keys[0].astype(jnp.float32) * gain).astype(jnp.bfloat16)

    def heads_view(array):
        return array.reshape(count_rows, H, HD)

    packed = jnp.concatenate(
        [
            heads_view(queries[0]),
            heads_view(scaled_keys),
            heads_view(values[0]),
            heads_view(d_out[0]),
        ],
        axis=2,
    ).transpose(1, 0, 2)
    cluster = cluster_ids[0].T
    owner = cluster // CPO
    label_value = (cluster % CPO + 1).astype(jnp.bfloat16)
    member = (owner[:, :, None] == jnp.arange(owners_count)[None, None, :]).astype(jnp.int32)
    earlier = jnp.cumsum(member, axis=1) - member
    position = jnp.sum(earlier * member, axis=2)
    target = owner * per_owner + position
    head_index = jnp.arange(H)[:, None]
    outbox = (
        jnp.zeros((H, owners_count * per_owner, 4 * HD), jnp.bfloat16)
        .at[head_index, target]
        .set(packed)
    )
    outbox = outbox.reshape(H, owners_count, per_owner, 4 * HD)
    labels = (
        jnp.zeros((H, owners_count * per_owner), jnp.bfloat16)
        .at[head_index, target]
        .set(label_value)
    )
    labels = labels.reshape(H, owners_count, per_owner)
    arrived = (
        lax.all_to_all(outbox, "seq", split_axis=1, concat_axis=1, tiled=True),
        lax.all_to_all(labels, "seq", split_axis=1, concat_axis=1, tiled=True),
    )
    returned = lax.all_to_all(owner_work(arrived), "seq", split_axis=1, concat_axis=1, tiled=True)
    gradient = returned.reshape(H, owners_count * per_owner, 3 * HD)[head_index, target].transpose(
        1, 0, 2
    )
    query_grad = gradient[:, :, :HD].reshape(count_rows, H * HD)
    scaled_grad = gradient[:, :, HD : 2 * HD].astype(jnp.float32)
    value_grad = gradient[:, :, 2 * HD :].reshape(count_rows, H * HD)
    key_grad = (gain_heads * scaled_grad).astype(jnp.bfloat16).reshape(count_rows, H * HD)
    partial_sum = jnp.sum(heads_view(keys[0]).astype(jnp.float32) * scaled_grad, axis=0).reshape(
        H * HD
    )
    gain_grad = lax.psum(partial_sum, ("dp", "seq"))
    return (query_grad[None], key_grad[None], value_grad[None], gain_grad)


def solution(mesh):
    in_specs = (
        P("dp", "seq", None),
        P("dp", "seq", None),
        P("dp", "seq", None),
        P("dp", "seq", None),
        P("dp", "seq", None),
        P(),
    )
    out_specs = (P("dp", "seq", None), P("dp", "seq", None), P("dp", "seq", None), P())
    return jax.shard_map(
        on_device, mesh=mesh, in_specs=in_specs, out_specs=out_specs, check_vma=False
    )
```

profile of v0, /device:TPU:1, one launch (start us, length us, event | category | flops | bytes accessed | tf_op | source)
XLA Modules:
  0.0 290.6 jit_solution(14743653222645183447)
XLA Ops:
  1.4 2.8 select_reduce_fusion
  4.3 0.8 or_bitcast_fusion
  5.1 0.7 multiply_reduce_fusion
  6.6 14.6 %scatter_custom_fusion = bf16[2048]{0:T(1024)(128)(2,1)S(1)} fusion(s32[2048]{0:T(1024)S(1)} %select_bitcast_fusion, bf16[2048]{0:T(1024)(128)(2,1)S(1)} %get-tuple-element.67, bf16[]{:T(256)} %constant.56.clone.1), kind=kCustom, calls=%fused_computation.70 | custom fusion | bytes 4098
  21.4 0.9 copy.123
  22.4 10.4 %all-to-all-start = ((bf16[16,32,4]{0,2,1:T(4,128)(2,1)}), bf16[16,32,4]{0,2,1:T(4,128)(2,1)S(1)}, u32[]{:S(2)}, u32[]{:S(2)}) async-start(bf16[16,32,4]{0,2,1:T(4,128)(2,1)} %copy.123), calls=%async_computation | async-start | bytes 65536 | tf_op jit(solution)/shard_map/all_to_all | solution.py:97
  32.7 1.1 convert_bitcast_fusion
  36.0 1.6 pad_maximum_fusion
  37.7 10.8 %scatter_custom_fusion.1 = bf16[2048,512]{1,0:T(8,128)(2,1)S(1)} fusion(s32[2048]{0:T(1024)S(1)} %select_bitcast_fusion, bf16[2048,512]{1,0:T(8,128)(2,1)} %bitcast.94, bf16[]{:T(256)} %constant.56.clone.1), kind=kCustom, calls=%fused_computation.44 | custom fusion | bytes 2097664
  48.5 2.1 reshape.50
  50.5 4.0 %copy.128 = bf16[16,32,4,512]{3,2,0,1:T(4,128)(2,1)} copy(bf16[16,32,4,512]{3,2,1,0:T(4,128)(2,1)} %reshape.50) | data formatting | bytes 4194304 | tf_op jit(solution)/shard_map/reshape | solution.py:88
  54.6 7.5 %all-to-all-start.1 = ((bf16[16,32,4,512]{3,2,0,1:T(4,128)(2,1)}), bf16[16,32,4,512]{3,2,0,1:T(4,128)(2,1)S(1)}, u32[]{:S(2)}, u32[]{:S(2)}) async-start(bf16[16,32,4,512]{3,2,0,1:T(4,128)(2,1)} %copy.128), calls=%async_computation.1 | async-start | bytes 4194304 | tf_op jit(solution)/shard_map/all_to_all | solution.py:96
  62.1 28.2 %all-to-all-done.1 = bf16[16,32,4,512]{3,2,0,1:T(4,128)(2,1)S(1)} async-done(((bf16[16,32,4,512]{3,2,0,1:T(4,128)(2,1)}), bf16[16,32,4,512]{3,2,0,1:T(4,128)(2,1)S(1)}, u32[]{:S(2)}, u32[]{:S(2)}) %all-to-all-start.1) | async-done | bytes 2097184 | tf_op jit(solution)/shard_map/all_to_all | solution.py:96
  90.4 2.0 copy.129
  92.3 3.5 %copy.131 = bf16[16,128,512]{1,2,0:T(8,128)(2,1)S(1)} copy(bf16[16,128,512]{2,0,1:T(8,128)(2,1)} %bitcast.89) | data formatting | bytes 4194304 | tf_op jit(solution)/shard_map/while | solution.py:46
  95.8 32.1 %while.10 = (s32[]{:T(128)}, bf16[16,128,384]{1,2,0:T(8,128)(2,1)}, bf16[16,128]{1,0:T(8,128)(2,1)S(1)}, bf16[16,128,512]{1,2,0:T(8,128)(2,1)S(1)}, s32[]{:T(128)}) while((s32[]{:T(128)}, bf16[16,128,384]{1,2,0:T(8,128)(2,1)}, bf16[16,128]{1,0:T(8,128)(2,1)S(1)}, bf16[16,128,512]{1,2,0:T(8,128)(2,1)S(1)}, s32[]{:T(128)}) %tuple.35), condition=%wide.region_8.9_spmd, body=%wide.region_4.8_spmd.sunk | while | flops 26328704 | bytes 1289029 | solution.py:46
  127.9 2.2 copy.132
  130.1 26.5 %all_to_all.15 = bf16[16,32,4,384]{3,0,2,1:T(8,128)(2,1)S(1)} all-to-all(bf16[16,32,4,384]{3,0,2,1:T(8,128)(2,1)S(1)} %bitcast.92), channel_id=1, replica_groups=mesh['dp'=16,'seq'=32] {'seq'}, dimensions={1} | all-to-all | bytes 3145728 | tf_op jit(solution)/shard_map/all_to_all | solution.py:99
  156.9 22.6 %gather_fusion = bf16[2048,384]{1,0:T(8,128)(2,1)} fusion(bf16[16,128,384]{2,1,0:T(8,128)(2,1)S(1)} %copy.139, s32[2048]{0:T(1024)S(1)} %get-tuple-element.59), kind=kCustom, calls=%fused_computation | custom fusion | bytes 3162112 | tf_op jit(solution)/shard_map/gather | solution.py:100
  179.6 1.6 fusion.28
  181.8 1.0 broadcast_in_dim_reshape.11
  182.8 105.1 %psum.7 = f32[2048]{0:T(1024)} all-reduce(f32[2048]{0:T(1024)S(1)} %bitcast.104), channel_id=1, replica_groups=mesh['dp'=16,'seq'=32] {'dp','seq'}, use_global_device_ids=true, to_apply=%region_10.11 | all-reduce | flops 2048 | bytes 16384 | tf_op jit(solution)/shard_map/psum | solution.py:110
  288.3 1.0 broadcast_in_dim_reshape.10
  289.6 1.0 broadcast_in_dim_reshape.12
  (193 shorter events, 37.4 us)
Async XLA Ops:
  4.2 29.9 %copy-start.1 = (bf16[1,128,2048]{2,1,0:T(8,128)(2,1)S(1)}, bf16[1,128,2048]{2,1,0:T(8,128)(2,1)}, u32[]{:S(2)}) copy-start(bf16[1,128,2048]{2,1,0:T(8,128)(2,1)} %param.8) | copy-start | bytes 1572868
  22.4 32.2 %all-to-all-start = ((bf16[16,32,4]{0,2,1:T(4,128)(2,1)}), bf16[16,32,4]{0,2,1:T(4,128)(2,1)S(1)}, u32[]{:S(2)}, u32[]{:S(2)}) async-start(bf16[16,32,4]{0,2,1:T(4,128)(2,1)} %copy.123), calls=%async_computation | async-start | bytes 65536 | tf_op jit(solution)/shard_map/all_to_all | solution.py:97
  33.9 1.0 copy-start.2
  34.1 1.1 copy-start.3
  34.9 0.7 copy-start.4
  54.6 35.8 %all-to-all-start.1 = ((bf16[16,32,4,512]{3,2,0,1:T(4,128)(2,1)}), bf16[16,32,4,512]{3,2,0,1:T(4,128)(2,1)S(1)}, u32[]{:S(2)}, u32[]{:S(2)}) async-start(bf16[16,32,4,512]{3,2,0,1:T(4,128)(2,1)} %copy.128), calls=%async_computation.1 | async-start | bytes 4194304 | tf_op jit(solution)/shard_map/all_to_all | solution.py:96
  179.6 1.6 copy-start
where the time goes:
time: 291 us
  blocking collectives  132 us (45%)
  local copies, waits for them, and re-layouts  69.9 us (24%)
  waiting for transfers between devices  28.2 us (10%)
  other arithmetic  22.8 us (8%)
  matrix products  19 us (7%)
  starting transfers between devices  17.9 us (6%)
    psum x1, blocking collectives, on_device(): gain_grad = lax.psum(partial_sum, ('dp', 'seq'))  105 us
    all_to_all x1, waiting for transfers between devices, on_device(): lax.all_to_all(outbox, 'seq', split_axis=1, concat_axis=1, tiled=True)  28.2 us
    unnamed x16, local copies, waits for them, and re-layouts  26.6 us
    all_to_all x1, blocking collectives, on_device(): lax.all_to_all(owner_work(arrived), 'seq', split_axis=1, concat_axis=1, t...  26.5 us
    gather x1, local copies, waits for them, and re-layouts, on_device(): returned.reshape(H, owners_count * per_owner, 3 * HD)[head_index, target]  22.6 us
    dynamic_update_slice x16, other arithmetic, owner_work(): lax.map(attend, (rows_in.reshape(heads_here, sources * depth, width), lab...  10.6 us
    all_to_all x1, starting transfers between devices, on_device(): lax.all_to_all(labels, 'seq', split_axis=1, concat_axis=1, tiled=True)  10.4 us
    all_to_all x1, starting transfers between devices, on_device(): lax.all_to_all(outbox, 'seq', split_axis=1, concat_axis=1, tiled=True)  7.49 us
  transfers between devices with their start and end apart: 2, of which 1 were waited for; matrix products, arithmetic and copies ran while one was open for 7% of the time, Pallas kernels for 0%

commit v1 on v0

v1 whole, which is shorter than its diff:
```python
import jax
import jax.numpy as jnp
from jax import lax
from jax.experimental import pallas as pl
from jax.experimental.pallas import tpu as pltpu
from jax.sharding import PartitionSpec as P

H = 16
HD = 128
CPO = 2
MOST = 4
TOK = 128
N_SEQ = 32
N_DP = 16
GH = 4
NG = H // GH
ROWS = N_SEQ * GH * MOST
MSG = GH * MOST
WIDE = 4 * HD
BACK = 3 * HD
MESH = pl.DeviceIdType.MESH
F32 = jnp.float32
BF16 = jnp.bfloat16
NEG = -1e30


def iota(shape, dim):
    return lax.broadcasted_iota(jnp.int32, shape, dim)


def dot(a, b):
    return lax.dot_general(a, b, (((1,), (0,)), ((), ())), preferred_element_type=F32)


def dot_nt(a, b):
    return lax.dot_general(a, b, (((1,), (1,)), ((), ())), preferred_element_type=F32)


def dot_tn(a, b):
    return lax.dot_general(a, b, (((0,), (0,)), ((), ())), preferred_element_type=F32)


def kernel(
    q_hbm, k_hbm, v_hbm, d_hbm, cid_hbm, gain_hbm,
    dq_hbm, dk_hbm, dv_hbm, gg_hbm,
    xin, cid_v, gain_v, place, back_place, outbox, inbox, ret_out, ret_in,
    lab_out, lab_in, rmat, dmat, out_v,
    gp, g_recv, g_mid, z_recv, g_row, g_fin,
    in_sem, small_sem, self_sem, ret_self_sem, lab_self_sem, g_self_sem,
    f_send, f_recv, b_send, b_recv, l_send, l_recv,
    g1_send, g1_recv, g2_send, g2_recv, g3_send, g3_recv, out_sem,
):
    me = lax.axis_index("seq")
    dp = lax.axis_index("dp")
    core = me % 2
    my = (me // 2) % 4
    mx = me // 8
    chip = me // 2

    def peer(k):
        dx, dy, dc = k // 8, (k // 2) % 4, k % 2
        return ((mx + dx) % 4) * 8 + ((my + dy) % 4) * 2 + (core + dc) % 2

    def loop(lo, hi, body):
        def step(i, carry):
            body(i)
            return carry

        lax.fori_loop(lo, hi, step, 0)

    barrier = pltpu.get_barrier_semaphore()
    loop(1, N_SEQ, lambda k: pl.semaphore_signal(
        barrier, inc=1, device_id=(dp, peer(k)), device_id_type=MESH))
    loop(1, N_DP, lambda k: pl.semaphore_signal(
        barrier, inc=1, device_id=((dp + k) % N_DP, me), device_id_type=MESH))

    cid_copy = pltpu.make_async_copy(cid_hbm.at[0], cid_v, small_sem.at[0])
    cid_copy.start()
    gain_copy = pltpu.make_async_copy(gain_hbm, gain_v, small_sem.at[1])
    gain_copy.start()

    def load(g):
        cols = pl.ds(pl.multiple_of(g * GH * HD, GH * HD), GH * HD)
        for t, ref in enumerate((q_hbm, k_hbm, v_hbm, d_hbm)):
            pltpu.make_async_copy(ref.at[0, :, cols], xin.at[g, t], in_sem.at[g]).start()

    loop(0, NG, load)
    cid_copy.wait()
    cid = cid_v[...].astype(F32).astype(BF16)

    def select(g):
        r = iota((ROWS, H), 0)
        return jnp.where(iota((ROWS, H), 1) == GH * g + (r // MOST) % GH, 1.0, 0.0).astype(BF16)

    def head_of(shape, dim):
        return (iota(shape, dim) // MOST) % GH

    def make_place(g):
        shape = (ROWS, TOK)
        r = iota(shape, 0)
        label = dot_nt(select(g), cid) - (CPO * (r // MSG)).astype(F32)
        member = (label == 0.0) | (label == 1.0)
        before = jnp.where(iota((TOK, TOK), 0) < iota((TOK, TOK), 1), 1.0, 0.0).astype(BF16)
        rank = dot(jnp.where(member, 1.0, 0.0).astype(BF16), before)
        chosen = member & (rank == (r % MOST).astype(F32))
        place[g] = jnp.where(chosen, 1.0, 0.0).astype(BF16)
        row_label = dot(
            jnp.where(chosen, label, 0.0).astype(BF16), jnp.ones((TOK, TOK), BF16)
        )
        spread = jnp.where(iota(shape, 1) == MSG * g + r % MSG, row_label, 0.0).astype(BF16)
        owners = jnp.where(
            iota((N_SEQ, ROWS), 1) // MSG == iota((N_SEQ, ROWS), 0), 1.0, 0.0
        ).astype(BF16)
        return dot(owners, spread)

    def make_back(g):
        shape = (TOK, ROWS)
        r = iota(shape, 1)
        label = dot_nt(cid, select(g)) - (CPO * (r // MSG)).astype(F32)
        member = (label == 0.0) | (label == 1.0)
        before = jnp.where(iota((TOK, TOK), 1) < iota((TOK, TOK), 0), 1.0, 0.0).astype(BF16)
        rank = dot(before, jnp.where(member, 1.0, 0.0).astype(BF16))
        chosen = member & (rank == (r % MOST).astype(F32))
        back_place[g] = jnp.where(chosen, 1.0, 0.0).astype(BF16)

    def pack(g):
        pltpu.make_async_copy(xin.at[g], xin.at[g], in_sem.at[g]).wait()
        head = head_of((ROWS, TOK), 0)
        chosen = place[g]
        zero = jnp.zeros_like(chosen)
        left = jnp.concatenate([jnp.where(head == h, chosen, zero) for h in range(GH)], axis=1)
        for t in range(4):
            stack = jnp.concatenate(
                [xin[g, t, :, h * HD : (h + 1) * HD] for h in range(GH)], axis=0
            )
            outbox[g, :, :, t * HD : (t + 1) * HD] = (
                dot(left, stack).astype(BF16).reshape(N_SEQ, MSG, HD)
            )

    def forward(g, k):
        to = peer(k)
        return pltpu.make_async_remote_copy(
            src_ref=outbox.at[g, to], dst_ref=inbox.at[g, me],
            send_sem=f_send.at[g], recv_sem=f_recv.at[g],
            device_id=(dp, to), device_id_type=MESH)

    def send_forward(g):
        loop(1, N_SEQ, lambda k: forward(g, k).start())
        pltpu.make_async_copy(outbox.at[g, me], inbox.at[g, me], self_sem.at[g]).start()

    def forward_all(g):
        return pltpu.make_async_remote_copy(
            src_ref=outbox.at[g, pl.ds(0, N_SEQ - 1)], dst_ref=inbox.at[g, pl.ds(0, N_SEQ - 1)],
            send_sem=f_send.at[g], recv_sem=f_recv.at[g],
            device_id=(dp, peer(1)), device_id_type=MESH)

    def back_all(g):
        return pltpu.make_async_remote_copy(
            src_ref=ret_out.at[g, pl.ds(0, N_SEQ - 1)], dst_ref=ret_in.at[g, pl.ds(0, N_SEQ - 1)],
            send_sem=b_send.at[g], recv_sem=b_recv.at[g],
            device_id=(dp, peer(1)), device_id_type=MESH)

    def label_all():
        return pltpu.make_async_remote_copy(
            src_ref=lab_out.at[pl.ds(0, N_SEQ - 1)], dst_ref=lab_in.at[pl.ds(0, N_SEQ - 1)],
            send_sem=l_send, recv_sem=l_recv,
            device_id=(dp, peer(1)), device_id_type=MESH)

    labels = make_place(0)
    pack(0)
    pl.semaphore_wait(barrier, N_SEQ - 1 + N_DP - 1)
    send_forward(0)

    labels = lax.fori_loop(1, NG, lambda g, acc: acc + make_place(g), labels)
    lab_out[...] = labels

    def send_label(k):
        to = peer(k)
        pltpu.make_async_remote_copy(
            src_ref=lab_out.at[pl.ds(to, 1)], dst_ref=lab_in.at[pl.ds(me, 1)],
            send_sem=l_send, recv_sem=l_recv,
            device_id=(dp, to), device_id_type=MESH).start()

    loop(1, N_SEQ, send_label)
    lab_self = pltpu.make_async_copy(
        lab_out.at[pl.ds(me, 1)], lab_in.at[pl.ds(me, 1)], lab_self_sem)
    lab_self.start()

    def pack_send(g):
        pack(g)
        send_forward(g)

    loop(1, NG, pack_send)
    loop(0, NG, make_back)
    gain_copy.wait()
    label_all().wait_recv()
    lab_self.wait()

    factor = HD ** (-0.5)

    def attend(g):
        forward_all(g).wait_recv()
        pltpu.make_async_copy(outbox.at[g, me], inbox.at[g, me], self_sem.at[g]).wait()
        shape = (ROWS, HD)
        r = iota(shape, 0)
        head = head_of(shape, 0)
        gain_rows = jnp.zeros(shape, F32)
        for h in range(GH):
            gain_rows = jnp.where(head == h, gain_v[pl.ds(GH * g + h, 1), :], gain_rows)
        from_src = jnp.where(
            iota((ROWS, N_SEQ), 0) // MSG == iota((ROWS, N_SEQ), 1), 1.0, 0.0
        ).astype(BF16)
        arrived = dot(from_src, lab_in[...].astype(BF16))
        arrived = jnp.where(iota(shape, 1) == MSG * g + r % MSG, arrived, 0.0).astype(BF16)
        code_col = dot(arrived, jnp.ones((HD, HD), BF16)) + (2 * head).astype(F32)
        code_row = dot_nt(jnp.ones((8, HD), BF16), arrived)[0:1, :] + (
            2 * head_of((1, ROWS), 1)
        ).astype(F32)

        def part(t, lo, hi):
            n = hi - lo
            return inbox[g, lo // MSG : hi // MSG, :, t * HD : (t + 1) * HD].reshape(n, HD)

        query = part(0, 0, ROWS)
        raw = part(1, 0, ROWS).astype(F32)
        value = part(2, 0, ROWS)
        upstream = part(3, 0, ROWS)
        scaled = (raw * gain_rows).astype(BF16)
        for i in range(GH):
            lo, hi = i * 128, (i + 1) * 128
            scores = dot_nt(scaled[:hi], query[lo:hi]) * factor
            allowed = (code_col[:hi] == code_row[:, lo:hi]) & (
                iota((hi, 128), 0) <= iota((hi, 128), 1) + lo
            )
            scores = jnp.where(allowed, scores, NEG)
            expo = jnp.exp(scores - jnp.max(scores, axis=0, keepdims=True))
            weights = expo * (1.0 / jnp.sum(expo, axis=0, keepdims=True))
            rounded = weights.astype(BF16)
            rmat[:hi, lo:hi] = rounded
            inner = dot_nt(value[:hi], upstream[lo:hi])
            delta = jnp.sum(rounded.astype(F32) * inner, axis=0, keepdims=True)
            grad = (weights * (inner - delta)).astype(BF16)
            dmat[:hi, lo:hi] = grad
            query_grad = (dot_tn(grad, scaled[:hi]) * factor).astype(BF16)
            ret_out[g, lo // MSG : hi // MSG, :, 0:HD] = query_grad.reshape(
                128 // MSG, MSG, HD)
        total = jnp.zeros((MSG, HD), F32)
        for j in range(GH):
            lo, hi = j * 128, (j + 1) * 128
            value_grad = dot(rmat[lo:hi, lo:], upstream[lo:]).astype(BF16)
            ret_out[g, lo // MSG : hi // MSG, :, 2 * HD : 3 * HD] = value_grad.reshape(
                128 // MSG, MSG, HD)
            scaled_grad = (dot(dmat[lo:hi, lo:], query[lo:]) * factor).astype(BF16).astype(F32)
            key_grad = (gain_rows[lo:hi] * scaled_grad).astype(BF16)
            ret_out[g, lo // MSG : hi // MSG, :, HD : 2 * HD] = key_grad.reshape(
                128 // MSG, MSG, HD)
            total = total + jnp.sum((raw[lo:hi] * scaled_grad).reshape(128 // MSG, MSG, HD), axis=0)

        def send_back(k):
            to = peer(k)
            pltpu.make_async_remote_copy(
                src_ref=ret_out.at[g, to], dst_ref=ret_in.at[g, me],
                send_sem=b_send.at[g], recv_sem=b_recv.at[g],
                device_id=(dp, to), device_id_type=MESH).start()

        loop(1, N_SEQ, send_back)
        pltpu.make_async_copy(ret_out.at[g, me], ret_in.at[g, me], ret_self_sem.at[g]).start()
        rows16 = iota((MSG, HD), 0) // MOST
        for h in range(GH):
            gp[pl.ds(GH * g + h, 1), :] = jnp.sum(
                jnp.where(rows16 == h, total, 0.0), axis=0, keepdims=True)

    loop(0, NG, attend)

    def gain_one(c):
        @pl.when(2 * c != me)
        def _():
            pltpu.make_async_remote_copy(
                src_ref=gp.at[pl.ds(c, 1)], dst_ref=g_recv.at[pl.ds(me, 1)],
                send_sem=g1_send, recv_sem=g1_recv,
                device_id=(dp, 2 * c), device_id_type=MESH).start()

    loop(0, H, gain_one)

    def unpack(g):
        back_all(g).wait_recv()
        pltpu.make_async_copy(ret_out.at[g, me], ret_in.at[g, me], ret_self_sem.at[g]).wait()
        head = head_of((TOK, ROWS), 1)
        chosen = back_place[g]
        zero = jnp.zeros_like(chosen)
        left = jnp.concatenate([jnp.where(head == h, chosen, zero) for h in range(GH)], axis=0)
        home = dot(left, ret_in[g].reshape(ROWS, BACK)).astype(BF16)
        cols = pl.ds(pl.multiple_of(g * GH * HD, GH * HD), GH * HD)
        for t, ref in enumerate((dq_hbm, dk_hbm, dv_hbm)):
            for h in range(GH):
                out_v[g, t, :, h * HD : (h + 1) * HD] = home[
                    h * TOK : (h + 1) * TOK, t * HD : (t + 1) * HD]
            pltpu.make_async_copy(out_v.at[g, t], ref.at[0, :, cols], out_sem.at[g]).start()

    def rows_copy(src, dst, n, send, recv):
        return pltpu.make_async_remote_copy(
            src_ref=src.at[pl.ds(0, n)], dst_ref=dst.at[pl.ds(0, n)], send_sem=send, recv_sem=recv,
            device_id=(dp, peer(1)), device_id_type=MESH)

    unpack(0)

    @pl.when(core == 0)
    def _():
        own = pltpu.make_async_copy(
            gp.at[pl.ds(chip, 1)], g_recv.at[pl.ds(me, 1)], g_self_sem.at[0])
        own.start()
        rows_copy(g_recv, g_recv, N_SEQ - 1, g1_send, g1_recv).wait_recv()
        own.wait()
        g_mid[...] = jnp.broadcast_to(jnp.sum(g_recv[...], axis=0, keepdims=True), g_mid.shape)

        def gain_two(k):
            pltpu.make_async_remote_copy(
                src_ref=g_mid.at[pl.ds(0, 1)], dst_ref=z_recv.at[pl.ds(dp, 1)],
                send_sem=g2_send, recv_sem=g2_recv,
                device_id=((dp + k) % N_DP, me), device_id_type=MESH).start()

        loop(1, N_DP, gain_two)
        pltpu.make_async_copy(
            g_mid.at[pl.ds(0, 1)], z_recv.at[pl.ds(dp, 1)], g_self_sem.at[1]).start()

    unpack(1)

    @pl.when(core == 0)
    def _():
        rows_copy(z_recv, z_recv, N_DP - 1, g2_send, g2_recv).wait()
        pltpu.make_async_copy(
            g_mid.at[pl.ds(0, 1)], z_recv.at[pl.ds(dp, 1)], g_self_sem.at[1]).wait()
        g_row[...] = jnp.broadcast_to(jnp.sum(z_recv[...], axis=0, keepdims=True), g_row.shape)

        def gain_three(k):
            pltpu.make_async_remote_copy(
                src_ref=g_row.at[pl.ds(0, 1)], dst_ref=g_fin.at[pl.ds(chip, 1)],
                send_sem=g3_send, recv_sem=g3_recv,
                device_id=(dp, peer(k)), device_id_type=MESH).start()

        loop(1, N_SEQ, gain_three)
        own = pltpu.make_async_copy(
            g_row.at[pl.ds(0, 1)], g_fin.at[pl.ds(chip, 1)], g_self_sem.at[0])
        own.start()
        own.wait()

    unpack(2)
    unpack(3)

    @pl.when(core == 0)
    def _():
        rows_copy(gp, gp, H - 1, g1_send, g1_recv).wait_send()
        rows_copy(g_fin, g_fin, H - 1, g3_send, g3_recv).wait_recv()
        rows_copy(g_recv, g_recv, N_SEQ - 1, g3_send, g3_recv).wait_send()

    @pl.when(core == 1)
    def _():
        rows_copy(gp, gp, H, g1_send, g1_recv).wait_send()
        rows_copy(g_fin, g_fin, H, g3_send, g3_recv).wait_recv()

    gain_out = pltpu.make_async_copy(g_fin, gg_hbm, small_sem.at[0])
    gain_out.start()

    def finish(g):
        forward_all(g).wait_send()
        back_all(g).wait_send()
        pltpu.make_async_copy(out_v.at[g], out_v.at[g], out_sem.at[g]).wait()

    loop(0, NG, finish)
    label_all().wait_send()
    gain_out.wait()


def on_device(queries, keys, values, d_out, cluster_ids, gain):
    anywhere = pl.BlockSpec(memory_space=pl.ANY)
    rows = jax.ShapeDtypeStruct(queries.shape, BF16)
    dma = pltpu.SemaphoreType.DMA
    query_grad, key_grad, value_grad, gain_grad = pl.pallas_call(
        kernel,
        out_shape=(rows, rows, rows, jax.ShapeDtypeStruct((H, HD), F32)),
        in_specs=[anywhere] * 6,
        out_specs=(anywhere,) * 4,
        scratch_shapes=[
            pltpu.VMEM((NG, 4, TOK, GH * HD), BF16),
            pltpu.VMEM((TOK, H), jnp.int32),
            pltpu.VMEM((H, HD), F32),
            pltpu.VMEM((NG, ROWS, TOK), BF16),
            pltpu.VMEM((NG, TOK, ROWS), BF16),
            pltpu.VMEM((NG, N_SEQ, MSG, WIDE), BF16),
            pltpu.VMEM((NG, N_SEQ, MSG, WIDE), BF16),
            pltpu.VMEM((NG, N_SEQ, MSG, BACK), BF16),
            pltpu.VMEM((NG, N_SEQ, MSG, BACK), BF16),
            pltpu.VMEM((N_SEQ, HD), F32),
            pltpu.VMEM((N_SEQ, HD), F32),
            pltpu.VMEM((ROWS, ROWS), BF16),
            pltpu.VMEM((ROWS, ROWS), BF16),
            pltpu.VMEM((NG, 3, TOK, GH * HD), BF16),
            pltpu.VMEM((H, HD), F32),
            pltpu.VMEM((N_SEQ, HD), F32),
            pltpu.VMEM((8, HD), F32),
            pltpu.VMEM((N_DP, HD), F32),
            pltpu.VMEM((8, HD), F32),
            pltpu.VMEM((H, HD), F32),
            dma((NG,)), dma((2,)), dma((NG,)), dma((NG,)), dma, dma((2,)),
            dma((NG,)), dma((NG,)), dma((NG,)), dma((NG,)), dma, dma,
            dma, dma, dma, dma, dma, dma, dma((NG,)),
        ],
        compiler_params=pltpu.CompilerParams(
            collective_id=0, has_side_effects=True, vmem_limit_bytes=48 * 2**20
        ),
    )(queries, keys, values, d_out, cluster_ids, gain.reshape(H, HD))
    return query_grad, key_grad, value_grad, gain_grad.reshape(H * HD)


def solution(mesh):
    rows = P("dp", "seq", None)
    return jax.shard_map(
        on_device, mesh=mesh, in_specs=(rows,) * 5 + (P(),),
        out_specs=(rows, rows, rows, P()), check_vma=False,
    )
```

time: 291 us -> 81.3 us (0.28)
  blocking collectives: 132 us -> 0 us
  Pallas kernels: 0 us -> 72.3 us
  local copies, waits for them, and re-layouts: 69.9 us -> 7.95 us
  waiting for transfers between devices: 28.2 us -> 0 us
  other arithmetic: 22.8 us -> 0 us
  matrix products: 19 us -> 0 us
  starting transfers between devices: 17.9 us -> 0 us
    psum x1 -> x0, blocking collectives: 105 us -> none  [on_device(): gain_grad = lax.psum(partial_sum, ('dp', 'seq'))]
    pallas_call x0 -> x1, Pallas kernels: none -> 72.3 us  [on_device(): pl.pallas_call(kernel, out_shape=(rows, rows, rows, jax.ShapeDtypeStruct(...]
    all_to_all x2 -> x0, waiting for transfers between devices: 28.2 us -> none  [the longest x1 28.2 us: on_device(): lax.all_to_all(outbox, 'seq', split_axis=1, concat_axis=1, tiled=True)]
    all_to_all x1 -> x0, blocking collectives: 26.5 us -> none  [on_device(): lax.all_to_all(owner_work(arrived), 'seq', split_axis=1, concat_axis=1, t...]
    gather x1 -> x0, local copies, waits for them, and re-layouts: 22.6 us -> none  [on_device(): returned.reshape(H, owners_count * per_owner, 3 * HD)[head_index, target]]
    dot_general x96 -> x0, matrix products: 19 us -> none  [the longest x16 3.76 us: attend(): jnp.dot(rounded.T, upstream, preferred_element_type=jnp.float32)]
    unnamed x16 -> x15, local copies, waits for them, and re-layouts: 26.6 us -> 7.95 us
    all_to_all x2 -> x0, starting transfers between devices: 17.9 us -> none  [the longest x1 10.4 us: on_device(): lax.all_to_all(labels, 'seq', split_axis=1, concat_axis=1, tiled=True)]
  transfers between devices with their start and end apart: 2 -> 0, of which waited for: 1 -> 0; matrix products, arithmetic and copies ran while one was open for 7% -> 0% of each run, Pallas kernels for 0% -> 0%
where the time goes in v1:
time: 81.3 us; the launch traced here: 81 us
  Pallas kernels  72.3 us (89%)
  local copies, waits for them, and re-layouts  7.95 us (10%)
    pallas_call x1, Pallas kernels, on_device(): pl.pallas_call(kernel, out_shape=(rows, rows, rows, jax.ShapeDtypeStruct(...  72.3 us
    unnamed x15, local copies, waits for them, and re-layouts  7.95 us

profile of v1, /device:TPU:1, one launch (start us, length us, event | category | flops | bytes accessed | tf_op | source)
XLA Modules:
  0.0 81.0 jit_solution(10317183531020359882)
XLA Ops:
  0.6 0.0 copy-start.4
  0.6 0.8 copy.10.cid_hbm
  1.4 0.0 copy-done.4
  1.4 0.0 copy-start
  1.5 1.0 %copy-done = bf16[1,128,2048]{2,1,0:T(8,128)(2,1)S(1)} copy-done((bf16[1,128,2048]{2,1,0:T(8,128)(2,1)S(1)}, bf16[1,128,2048]{2,1,0:T(8,128)(2,1)}, u32[]{:S(2)}) %copy-start) | copy-done | bytes 524312
  2.5 0.0 copy-start.1
  2.5 1.0 %copy-done.1 = bf16[1,128,2048]{2,1,0:T(8,128)(2,1)S(1)} copy-done((bf16[1,128,2048]{2,1,0:T(8,128)(2,1)S(1)}, bf16[1,128,2048]{2,1,0:T(8,128)(2,1)}, u32[]{:S(2)}) %copy-start.1) | copy-done | bytes 524312
  3.5 0.0 copy-start.2
  3.5 1.0 %copy-done.2 = bf16[1,128,2048]{2,1,0:T(8,128)(2,1)S(1)} copy-done((bf16[1,128,2048]{2,1,0:T(8,128)(2,1)S(1)}, bf16[1,128,2048]{2,1,0:T(8,128)(2,1)}, u32[]{:S(2)}) %copy-start.2) | copy-done | bytes 524312
  4.6 0.0 copy-start.3
  4.6 1.0 %copy-done.3 = bf16[1,128,2048]{2,1,0:T(8,128)(2,1)S(1)} copy-done((bf16[1,128,2048]{2,1,0:T(8,128)(2,1)S(1)}, bf16[1,128,2048]{2,1,0:T(8,128)(2,1)}, u32[]{:S(2)}) %copy-start.3) | copy-done | bytes 524312
  5.6 72.3 %shard_map.93 = (bf16[1,128,2048]{2,1,0:T(8,128)(2,1)S(1)}, bf16[1,128,2048]{2,1,0:T(8,128)(2,1)S(1)}, bf16[1,128,2048]{2,1,0:T(8,128)(2,1)S(1)}, f32[16,128]{1,0:T(8,128)S(1)}) custom-call(bf16[1,128,2048]{2,1,0:T(8,128)(2,1)S(1)} %copy-done, bf16[1,128,2048]{2,1,0:T(8,128)(2,1)S(1)} %copy-done.1, bf16[1,128,2048]{2,1,0:T(8,128)(2,1)S(1)} %copy-done.2, ...), custom_call_target="tpu_custom_call" | custom-call | tf_op jit(solution)/shard_map/pallas_call | solution.py:378
  78.0 0.8 copy.15
  78.8 0.8 copy.16
  79.6 0.8 copy.17
  80.4 0.6 copy.18
Async XLA Ops:
  0.6 0.8 %copy-start.4 = (f32[2048]{0:T(1024)S(1)}, f32[2048]{0:T(1024)}, u32[]{:S(2)}) copy-start(f32[2048]{0:T(1024)} %param.11) | copy-start | bytes 24580
  1.4 1.0 %copy-start = (bf16[1,128,2048]{2,1,0:T(8,128)(2,1)S(1)}, bf16[1,128,2048]{2,1,0:T(8,128)(2,1)}, u32[]{:S(2)}) copy-start(bf16[1,128,2048]{2,1,0:T(8,128)(2,1)} %q_hbm.1) | copy-start | bytes 1572868
  2.5 1.0 %copy-start.1 = (bf16[1,128,2048]{2,1,0:T(8,128)(2,1)S(1)}, bf16[1,128,2048]{2,1,0:T(8,128)(2,1)}, u32[]{:S(2)}) copy-start(bf16[1,128,2048]{2,1,0:T(8,128)(2,1)} %k_hbm.1) | copy-start | bytes 1572868
  3.5 1.0 %copy-start.2 = (bf16[1,128,2048]{2,1,0:T(8,128)(2,1)S(1)}, bf16[1,128,2048]{2,1,0:T(8,128)(2,1)}, u32[]{:S(2)}) copy-start(bf16[1,128,2048]{2,1,0:T(8,128)(2,1)} %v_hbm.1) | copy-start | bytes 1572868
  4.6 1.0 %copy-start.3 = (bf16[1,128,2048]{2,1,0:T(8,128)(2,1)S(1)}, bf16[1,128,2048]{2,1,0:T(8,128)(2,1)}, u32[]{:S(2)}) copy-start(bf16[1,128,2048]{2,1,0:T(8,128)(2,1)} %d_hbm.1) | copy-start | bytes 1572868

commit v2 on v1

--- a/solution.py
+++ b/solution.py
@@ -41,14 +41,14 @@
 
 
 def kernel(
-    q_hbm, k_hbm, v_hbm, d_hbm, cid_hbm, gain_hbm,
-    dq_hbm, dk_hbm, dv_hbm, gg_hbm,
-    xin, cid_v, gain_v, place, back_place, outbox, inbox, ret_out, ret_in,
-    lab_out, lab_in, rmat, dmat, out_v,
-    gp, g_recv, g_mid, z_recv, g_row, g_fin,
-    in_sem, small_sem, self_sem, ret_self_sem, lab_self_sem, g_self_sem,
+    q_hbm, k_hbm, v_hbm, d_hbm, cid_hbm, gain_v,
+    dq_ref, dk_ref, dv_ref, gg_ref,
+    xin, cid_v, place, back_place, outbox, inbox, ret_out, ret_in,
+    lab_out, lab_in, rmat, dmat,
+    gp, c_in, chip_sum, z_in, z_sum, p_in,
+    in_sem, small_sem, self_sem, ret_self_sem, lab_self_sem, go_sem,
     f_send, f_recv, b_send, b_recv, l_send, l_recv,
-    g1_send, g1_recv, g2_send, g2_recv, g3_send, g3_recv, out_sem,
+    c_send, c_recv, z_send, z_recv, p_send, p_recv,
 ):
     me = lax.axis_index("seq")
     dp = lax.axis_index("dp")
@@ -69,15 +69,22 @@
         lax.fori_loop(lo, hi, step, 0)
 
     barrier = pltpu.get_barrier_semaphore()
-    loop(1, N_SEQ, lambda k: pl.semaphore_signal(
-        barrier, inc=1, device_id=(dp, peer(k)), device_id_type=MESH))
-    loop(1, N_DP, lambda k: pl.semaphore_signal(
-        barrier, inc=1, device_id=((dp + k) % N_DP, me), device_id_type=MESH))
-
-    cid_copy = pltpu.make_async_copy(cid_hbm.at[0], cid_v, small_sem.at[0])
+    sibling = (dp, chip * 2 + 1 - core)
+
+    def greet_plane(c):
+        @pl.when(2 * c != me)
+        def _():
+            pl.semaphore_signal(barrier, inc=1, device_id=(dp, 2 * c), device_id_type=MESH)
+
+    loop(0, N_SEQ // 2, greet_plane)
+
+    @pl.when(core == 1)
+    def _():
+        loop(1, N_DP, lambda k: pl.semaphore_signal(
+            barrier, inc=1, device_id=((dp + k) % N_DP, me), device_id_type=MESH))
+
+    cid_copy = pltpu.make_async_copy(cid_hbm.at[0], cid_v, small_sem)
     cid_copy.start()
-    gain_copy = pltpu.make_async_copy(gain_hbm, gain_v, small_sem.at[1])
-    gain_copy.start()
 
     def load(g):
         cols = pl.ds(pl.multiple_of(g * GH * HD, GH * HD), GH * HD)
@@ -92,13 +99,17 @@
         r = iota((ROWS, H), 0)
         return jnp.where(iota((ROWS, H), 1) == GH * g + (r // MOST) % GH, 1.0, 0.0).astype(BF16)
 
+    def select_back(g):
+        r = iota((H, ROWS), 1)
+        return jnp.where(iota((H, ROWS), 0) == GH * g + (r // MOST) % GH, 1.0, 0.0).astype(BF16)
+
     def head_of(shape, dim):
         return (iota(shape, dim) // MOST) % GH
 
     def make_place(g):
         shape = (ROWS, TOK)
         r = iota(shape, 0)
-        label = dot_nt(select(g), cid) - (CPO * (r // MSG)).astype(F32)
+        label = dot(select(g), cid) - (CPO * (r // MSG)).astype(F32)
         member = (label == 0.0) | (label == 1.0)
         before = jnp.where(iota((TOK, TOK), 0) < iota((TOK, TOK), 1), 1.0, 0.0).astype(BF16)
         rank = dot(jnp.where(member, 1.0, 0.0).astype(BF16), before)
@@ -116,7 +127,7 @@
     def make_back(g):
         shape = (TOK, ROWS)
         r = iota(shape, 1)
-        label = dot_nt(cid, select(g)) - (CPO * (r // MSG)).astype(F32)
+        label = dot_tn(cid, select_back(g)) - (CPO * (r // MSG)).astype(F32)
         member = (label == 0.0) | (label == 1.0)
         before = jnp.where(iota((TOK, TOK), 1) < iota((TOK, TOK), 0), 1.0, 0.0).astype(BF16)
         rank = dot(before, jnp.where(member, 1.0, 0.0).astype(BF16))
@@ -168,7 +179,16 @@
 
     labels = make_place(0)
     pack(0)
-    pl.semaphore_wait(barrier, N_SEQ - 1 + N_DP - 1)
+
+    @pl.when(core == 0)
+    def _():
+        pl.semaphore_wait(barrier, N_SEQ - 1)
+        pl.semaphore_signal(go_sem, inc=1, device_id=sibling, device_id_type=MESH)
+
+    @pl.when(core == 1)
+    def _():
+        pl.semaphore_wait(go_sem, 1)
+
     send_forward(0)
 
     labels = lax.fori_loop(1, NG, lambda g, acc: acc + make_place(g), labels)
@@ -192,13 +212,60 @@
 
     loop(1, NG, pack_send)
     loop(0, NG, make_back)
-    gain_copy.wait()
     label_all().wait_recv()
     lab_self.wait()
 
     factor = HD ** (-0.5)
 
+    def chip_copy(n):
+        return pltpu.make_async_remote_copy(
+            src_ref=gp.at[n], dst_ref=c_in.at[n], send_sem=c_send.at[n], recv_sem=c_recv.at[n],
+            device_id=sibling, device_id_type=MESH)
+
+    def gain_along(n):
+        chip_copy(n).wait_recv()
+        chip_sum[n] = gp[n] + c_in[n]
+        z_in[n, dp] = chip_sum[n]
+
+        def send(k):
+            pltpu.make_async_remote_copy(
+                src_ref=chip_sum.at[n], dst_ref=z_in.at[n, dp],
+                send_sem=z_send.at[n], recv_sem=z_recv.at[n],
+                device_id=((dp + k) % N_DP, me), device_id_type=MESH).start()
+
+        loop(1, N_DP, send)
+
+    def along_all(n):
+        return pltpu.make_async_remote_copy(
+            src_ref=z_in.at[n, pl.ds(0, N_DP - 1)], dst_ref=z_in.at[n, pl.ds(0, N_DP - 1)],
+            send_sem=z_send.at[n], recv_sem=z_recv.at[n],
+            device_id=sibling, device_id_type=MESH)
+
+    def gain_plane(n):
+        along_all(n).wait_recv()
+        z_sum[n] = jnp.sum(z_in[n], axis=0)
+        p_in[n, chip] = z_sum[n]
+
+        def send(k):
+            pltpu.make_async_remote_copy(
+                src_ref=z_sum.at[n], dst_ref=p_in.at[n, chip],
+                send_sem=p_send.at[n], recv_sem=p_recv.at[n],
+                device_id=(dp, peer(k)), device_id_type=MESH).start()
+
+        loop(1, N_SEQ, send)
+
+    def plane_all(n, count):
+        return pltpu.make_async_remote_copy(
+            src_ref=p_in.at[n, pl.ds(0, count)], dst_ref=p_in.at[n, pl.ds(0, count)],
+            send_sem=p_send.at[n], recv_sem=p_recv.at[n],
+            device_id=sibling, device_id_type=MESH)
+
     def attend(g):
+        @pl.when((g == 3) & (core == 1))
+        def _():
+            pl.semaphore_wait(barrier, N_DP - 1)
+            gain_along(0)
+
         forward_all(g).wait_recv()
         pltpu.make_async_copy(outbox.at[g, me], inbox.at[g, me], self_sem.at[g]).wait()
         shape = (ROWS, HD)
@@ -256,6 +323,19 @@
                 128 // MSG, MSG, HD)
             total = total + jnp.sum((raw[lo:hi] * scaled_grad).reshape(128 // MSG, MSG, HD), axis=0)
 
+        rows16 = iota((MSG, HD), 0) // MOST
+        for h in range(GH):
+            gp[g // 2, pl.ds(GH * (g % 2) + h, 1), :] = jnp.sum(
+                jnp.where(rows16 == h, total, 0.0), axis=0, keepdims=True)
+
+        @pl.when((g % 2 == 1) & (core == 0))
+        def _():
+            chip_copy(g // 2).start()
+
+        @pl.when((g == 3) & (core == 1))
+        def _():
+            gain_along(1)
+
         def send_back(k):
             to = peer(k)
             pltpu.make_async_remote_copy(
@@ -265,22 +345,8 @@
 
         loop(1, N_SEQ, send_back)
         pltpu.make_async_copy(ret_out.at[g, me], ret_in.at[g, me], ret_self_sem.at[g]).start()
-        rows16 = iota((MSG, HD), 0) // MOST
-        for h in range(GH):
-            gp[pl.ds(GH * g + h, 1), :] = jnp.sum(
-                jnp.where(rows16 == h, total, 0.0), axis=0, keepdims=True)
 
     loop(0, NG, attend)
-
-    def gain_one(c):
-        @pl.when(2 * c != me)
-        def _():
-            pltpu.make_async_remote_copy(
-                src_ref=gp.at[pl.ds(c, 1)], dst_ref=g_recv.at[pl.ds(me, 1)],
-                send_sem=g1_send, recv_sem=g1_recv,
-                device_id=(dp, 2 * c), device_id_type=MESH).start()
-
-    loop(0, H, gain_one)
 
     def unpack(g):
         back_all(g).wait_recv()
@@ -290,100 +356,74 @@
         zero = jnp.zeros_like(chosen)
         left = jnp.concatenate([jnp.where(head == h, chosen, zero) for h in range(GH)], axis=0)
         home = dot(left, ret_in[g].reshape(ROWS, BACK)).astype(BF16)
-        cols = pl.ds(pl.multiple_of(g * GH * HD, GH * HD), GH * HD)
-        for t, ref in enumerate((dq_hbm, dk_hbm, dv_hbm)):
+        for t, ref in enumerate((dq_ref, dk_ref, dv_ref)):
             for h in range(GH):
-                out_v[g, t, :, h * HD : (h + 1) * HD] = home[
-                    h * TOK : (h + 1) * TOK, t * HD : (t + 1) * HD]
-            pltpu.make_async_copy(out_v.at[g, t], ref.at[0, :, cols], out_sem.at[g]).start()
-
-    def rows_copy(src, dst, n, send, recv):
-        return pltpu.make_async_remote_copy(
-            src_ref=src.at[pl.ds(0, n)], dst_ref=dst.at[pl.ds(0, n)], send_sem=send, recv_sem=recv,
-            device_id=(dp, peer(1)), device_id_type=MESH)
+                cols = pl.ds(pl.multiple_of((g * GH + h) * HD, HD), HD)
+                ref[0, :, cols] = home[h * TOK : (h + 1) * TOK, t * HD : (t + 1) * HD]
+
+    @pl.when(core == 1)
+    def _():
+        gain_plane(0)
 
     unpack(0)
 
-    @pl.when(core == 0)
-    def _():
-        own = pltpu.make_async_copy(
-            gp.at[pl.ds(chip, 1)], g_recv.at[pl.ds(me, 1)], g_self_sem.at[0])
-        own.start()
-        rows_copy(g_recv, g_recv, N_SEQ - 1, g1_send, g1_recv).wait_recv()
-        own.wait()
-        g_mid[...] = jnp.broadcast_to(jnp.sum(g_recv[...], axis=0, keepdims=True), g_mid.shape)
-
-        def gain_two(k):
-            pltpu.make_async_remote_copy(
-                src_ref=g_mid.at[pl.ds(0, 1)], dst_ref=z_recv.at[pl.ds(dp, 1)],
-                send_sem=g2_send, recv_sem=g2_recv,
-                device_id=((dp + k) % N_DP, me), device_id_type=MESH).start()
-
-        loop(1, N_DP, gain_two)
-        pltpu.make_async_copy(
-            g_mid.at[pl.ds(0, 1)], z_recv.at[pl.ds(dp, 1)], g_self_sem.at[1]).start()
+    @pl.when(core == 1)
+    def _():
+        gain_plane(1)
 
     unpack(1)
-
-    @pl.when(core == 0)
-    def _():
-        rows_copy(z_recv, z_recv, N_DP - 1, g2_send, g2_recv).wait()
-        pltpu.make_async_copy(
-            g_mid.at[pl.ds(0, 1)], z_recv.at[pl.ds(dp, 1)], g_self_sem.at[1]).wait()
-        g_row[...] = jnp.broadcast_to(jnp.sum(z_recv[...], axis=0, keepdims=True), g_row.shape)
-
-        def gain_three(k):
-            pltpu.make_async_remote_copy(
-                src_ref=g_row.at[pl.ds(0, 1)], dst_ref=g_fin.at[pl.ds(chip, 1)],
-                send_sem=g3_send, recv_sem=g3_recv,
-                device_id=(dp, peer(k)), device_id_type=MESH).start()
-
-        loop(1, N_SEQ, gain_three)
-        own = pltpu.make_async_copy(
-            g_row.at[pl.ds(0, 1)], g_fin.at[pl.ds(chip, 1)], g_self_sem.at[0])
-        own.start()
-        own.wait()
-
     unpack(2)
     unpack(3)
 
     @pl.when(core == 0)
     def _():
-        rows_copy(gp, gp, H - 1, g1_send, g1_recv).wait_send()
-        rows_copy(g_fin, g_fin, H - 1, g3_send, g3_recv).wait_recv()
-        rows_copy(g_recv, g_recv, N_SEQ - 1, g3_send, g3_recv).wait_send()
+        for n in range(2):
+            plane_all(n, N_SEQ // 2).wait_recv()
+            chip_copy(n).wait_send()
 
     @pl.when(core == 1)
     def _():
-        rows_copy(gp, gp, H, g1_send, g1_recv).wait_send()
-        rows_copy(g_fin, g_fin, H, g3_send, g3_recv).wait_recv()
-
-    gain_out = pltpu.make_async_copy(g_fin, gg_hbm, small_sem.at[0])
-    gain_out.start()
+        for n in range(2):
+            plane_all(n, N_SEQ // 2 - 1).wait_recv()
+            along_all(n).wait_send()
+            plane_all(n, N_SEQ // 2 - 1).wait_send()
+            plane_all(n, N_SEQ // 2).wait_send()
+
+    for n in range(2):
+        gg_ref[n * 8 : (n + 1) * 8, :] = jnp.sum(p_in[n], axis=0)
 
     def finish(g):
         forward_all(g).wait_send()
         back_all(g).wait_send()
-        pltpu.make_async_copy(out_v.at[g], out_v.at[g], out_sem.at[g]).wait()
 
     loop(0, NG, finish)
     label_all().wait_send()
-    gain_out.wait()
+
+
+def hand_over(a, b, c, d, oa, ob, oc, od, sem):
+    copies = [
+        pltpu.make_async_copy(src, dst, sem.at[i])
+        for i, (src, dst) in enumerate(zip((a, b, c, d), (oa, ob, oc, od)))
+    ]
+    for copy in copies:
+        copy.start()
+    for copy in copies:
+        copy.wait()
 
 
 def on_device(queries, keys, values, d_out, cluster_ids, gain):
     anywhere = pl.BlockSpec(memory_space=pl.ANY)
+    in_vmem = pl.BlockSpec(memory_space=pltpu.VMEM)
     rows = jax.ShapeDtypeStruct(queries.shape, BF16)
     dma = pltpu.SemaphoreType.DMA
     query_grad, key_grad, value_grad, gain_grad = pl.pallas_call(
         kernel,
         out_shape=(rows, rows, rows, jax.ShapeDtypeStruct((H, HD), F32)),
-        in_specs=[anywhere] * 6,
-        out_specs=(anywhere,) * 4,
+        in_specs=[anywhere] * 5 + [in_vmem],
+        out_specs=(in_vmem,) * 4,
         scratch_shapes=[
             pltpu.VMEM((NG, 4, TOK, GH * HD), BF16),
-            pltpu.VMEM((TOK, H), jnp.int32),
-            pltpu.VMEM((H, HD), F32),
+            pltpu.VMEM((H, TOK), jnp.int32),
             pltpu.VMEM((NG, ROWS, TOK), BF16),
             pltpu.VMEM((NG, TOK, ROWS), BF16),
             pltpu.VMEM((NG, N_SEQ, MSG, WIDE), BF16),
@@ -394,21 +434,28 @@
             pltpu.VMEM((N_SEQ, HD), F32),
             pltpu.VMEM((ROWS, ROWS), BF16),
             pltpu.VMEM((ROWS, ROWS), BF16),
-            pltpu.VMEM((NG, 3, TOK, GH * HD), BF16),
-            pltpu.VMEM((H, HD), F32),
-            pltpu.VMEM((N_SEQ, HD), F32),
-            pltpu.VMEM((8, HD), F32),
-            pltpu.VMEM((N_DP, HD), F32),
-            pltpu.VMEM((8, HD), F32),
-            pltpu.VMEM((H, HD), F32),
-            dma((NG,)), dma((2,)), dma((NG,)), dma((NG,)), dma, dma((2,)),
+            pltpu.VMEM((2, 8, HD), F32),
+            pltpu.VMEM((2, 8, HD), F32),
+            pltpu.VMEM((2, 8, HD), F32),
+            pltpu.VMEM((2, N_DP, 8, HD), F32),
+            pltpu.VMEM((2, 8, HD), F32),
+            pltpu.VMEM((2, N_SEQ // 2, 8, HD), F32),
+            dma((NG,)), dma, dma((NG,)), dma((NG,)), dma, pltpu.SemaphoreType.REGULAR,
             dma((NG,)), dma((NG,)), dma((NG,)), dma((NG,)), dma, dma,
-            dma, dma, dma, dma, dma, dma, dma((NG,)),
+            dma((2,)), dma((2,)), dma((2,)), dma((2,)), dma((2,)), dma((2,)),
         ],
         compiler_params=pltpu.CompilerParams(
-            collective_id=0, has_side_effects=True, vmem_limit_bytes=48 * 2**20
+            collective_id=0, has_side_effects=True, vmem_limit_bytes=52 * 2**20
         ),
-    )(queries, keys, values, d_out, cluster_ids, gain.reshape(H, HD))
+    )(queries, keys, values, d_out, cluster_ids.swapaxes(1, 2), gain.reshape(H, HD))
+    query_grad, key_grad, value_grad, gain_grad = pl.pallas_call(
+        hand_over,
+        out_shape=(rows, rows, rows, jax.ShapeDtypeStruct((H, HD), F32)),
+        in_specs=[in_vmem] * 4,
+        out_specs=(anywhere,) * 4,
+        scratch_shapes=[dma((4,))],
+        compiler_params=pltpu.CompilerParams(vmem_limit_bytes=4 * 2**20),
+    )(query_grad, key_grad, value_grad, gain_grad)
     return query_grad, key_grad, value_grad, gain_grad.reshape(H * HD)
 
 

time: 81.3 us -> 61.7 us (0.76)
  Pallas kernels: 72.3 us -> 59.5 us
  local copies, waits for them, and re-layouts: 7.95 us -> 1.39 us
    pallas_call x1, Pallas kernels: 72.3 us -> 58.3 us  [on_device(): pl.pallas_call(kernel, out_shape=(rows, rows, rows, jax.ShapeDtypeStruct(...]
    unnamed x15 -> x4, local copies, waits for them, and re-layouts: 7.95 us -> 1.39 us
    pallas_call x0 -> x1, Pallas kernels: none -> 1.18 us  [on_device(): pl.pallas_call(hand_over, out_shape=(rows, rows, rows, jax.ShapeDtypeStru...]
where the time goes in v2:
time: 61.7 us; the launch traced here: 61.5 us
  Pallas kernels  59.5 us (96%)
  local copies, waits for them, and re-layouts  1.39 us (2%)
  between operations  0.65 us (1%)
    pallas_call x1, Pallas kernels, on_device(): pl.pallas_call(kernel, out_shape=(rows, rows, rows, jax.ShapeDtypeStruct(...  58.3 us
    unnamed x4, local copies, waits for them, and re-layouts  1.39 us

profile of v2, /device:TPU:1, one launch (start us, length us, event | category | flops | bytes accessed | tf_op | source)
XLA Modules:
  0.0 61.5 jit_solution(10705401247760864208)
XLA Ops:
  0.6 0.0 copy-start
  0.6 0.7 %copy-done = s32[1,128,16]{1,2,0:T(8,128)S(1)} copy-done((s32[1,128,16]{1,2,0:T(8,128)S(1)}, s32[1,128,16]{1,2,0:T(8,128)}, u32[]{:S(2)}) %copy-start) | copy-done | bytes 8216
  1.3 0.0 copy-start.1
  1.3 0.7 %copy-done.1 = f32[2048]{0:T(1024)S(1)} copy-done((f32[2048]{0:T(1024)S(1)}, f32[2048]{0:T(1024)}, u32[]{:S(2)}) %copy-start.1) | copy-done | bytes 8216
  2.0 58.3 %shard_map.93 = (bf16[1,128,2048]{2,1,0:T(8,128)(2,1)S(1)}, bf16[1,128,2048]{2,1,0:T(8,128)(2,1)S(1)}, bf16[1,128,2048]{2,1,0:T(8,128)(2,1)S(1)}, f32[16,128]{1,0:T(8,128)S(1)}) custom-call(bf16[1,128,2048]{2,1,0:T(8,128)(2,1)} %q_hbm.1, bf16[1,128,2048]{2,1,0:T(8,128)(2,1)} %k_hbm.1, bf16[1,128,2048]{2,1,0:T(8,128)(2,1)} %v_hbm.1, ...), custom_call_target="tpu_custom_call" | custom-call | tf_op jit(solution)/shard_map/pallas_call | solution.py:419
  60.3 1.2 %shard_map.94 = (bf16[1,128,2048]{2,1,0:T(8,128)(2,1)}, bf16[1,128,2048]{2,1,0:T(8,128)(2,1)}, bf16[1,128,2048]{2,1,0:T(8,128)(2,1)}, f32[16,128]{1,0:T(8,128)}) custom-call(bf16[1,128,2048]{2,1,0:T(8,128)(2,1)S(1)} %get-tuple-element.12.a, bf16[1,128,2048]{2,1,0:T(8,128)(2,1)S(1)} %get-tuple-element.13.b, bf16[1,128,2048]{2,1,0:T(8,128)(2,1)S(1)} %get-tuple-element.14.c, ...), custom_call_target="tpu_custom_call" | custom-call | tf_op jit(solution)/shard_map/pallas_call | solution.py:451
Async XLA Ops:
  0.6 0.7 %copy-start = (s32[1,128,16]{1,2,0:T(8,128)S(1)}, s32[1,128,16]{1,2,0:T(8,128)}, u32[]{:S(2)}) copy-start(s32[1,128,16]{1,2,0:T(8,128)} %param.10) | copy-start | bytes 24580
  1.3 0.7 %copy-start.1 = (f32[2048]{0:T(1024)S(1)}, f32[2048]{0:T(1024)}, u32[]{:S(2)}) copy-start(f32[2048]{0:T(1024)} %param.11) | copy-start | bytes 24580

commit v3 on v2

--- a/solution.py
+++ b/solution.py
@@ -419,7 +419,7 @@
     query_grad, key_grad, value_grad, gain_grad = pl.pallas_call(
         kernel,
         out_shape=(rows, rows, rows, jax.ShapeDtypeStruct((H, HD), F32)),
-        in_specs=[anywhere] * 5 + [in_vmem],
+        in_specs=[anywhere] * 4 + [pl.BlockSpec(memory_space=pltpu.HBM), in_vmem],
         out_specs=(in_vmem,) * 4,
         scratch_shapes=[
             pltpu.VMEM((NG, 4, TOK, GH * HD), BF16),
@@ -447,7 +447,7 @@
         compiler_params=pltpu.CompilerParams(
             collective_id=0, has_side_effects=True, vmem_limit_bytes=52 * 2**20
         ),
-    )(queries, keys, values, d_out, cluster_ids.swapaxes(1, 2), gain.reshape(H, HD))
+    )(queries, keys, values, d_out, pltpu.with_memory_space_constraint(cluster_ids.swapaxes(1, 2), pltpu.HBM), pltpu.with_memory_space_constraint(gain.reshape(H, HD), pltpu.HBM))
     query_grad, key_grad, value_grad, gain_grad = pl.pallas_call(
         hand_over,
         out_shape=(rows, rows, rows, jax.ShapeDtypeStruct((H, HD), F32)),

time: 61.7 us -> 60.6 us (0.982)
  local copies, waits for them, and re-layouts: 1.39 us -> 0 us
    unnamed x4 -> x0, local copies, waits for them, and re-layouts: 1.39 us -> none
where the time goes in v3:
time: 60.6 us; the launch traced here: 60.4 us
  Pallas kernels  59.7 us (99%)
  between operations  0.64 us (1%)
    pallas_call x1, Pallas kernels, on_device(): pl.pallas_call(kernel, out_shape=(rows, rows, rows, jax.ShapeDtypeStruct(...  58.5 us

profile of v3, /device:TPU:1, one launch (start us, length us, event | category | flops | bytes accessed | tf_op | source)
XLA Modules:
  0.0 60.4 jit_solution(12517503575186932219)
XLA Ops:
  0.6 58.5 %shard_map.93 = (bf16[1,128,2048]{2,1,0:T(8,128)(2,1)S(1)}, bf16[1,128,2048]{2,1,0:T(8,128)(2,1)S(1)}, bf16[1,128,2048]{2,1,0:T(8,128)(2,1)S(1)}, f32[16,128]{1,0:T(8,128)S(1)}) custom-call(bf16[1,128,2048]{2,1,0:T(8,128)(2,1)} %q_hbm.1, bf16[1,128,2048]{2,1,0:T(8,128)(2,1)} %k_hbm.1, bf16[1,128,2048]{2,1,0:T(8,128)(2,1)} %v_hbm.1, ...), custom_call_target="tpu_custom_call" | custom-call | tf_op jit(solution)/shard_map/pallas_call | solution.py:419
  59.2 1.2 %shard_map.94 = (bf16[1,128,2048]{2,1,0:T(8,128)(2,1)}, bf16[1,128,2048]{2,1,0:T(8,128)(2,1)}, bf16[1,128,2048]{2,1,0:T(8,128)(2,1)}, f32[16,128]{1,0:T(8,128)}) custom-call(bf16[1,128,2048]{2,1,0:T(8,128)(2,1)S(1)} %get-tuple-element.12.a, bf16[1,128,2048]{2,1,0:T(8,128)(2,1)S(1)} %get-tuple-element.13.b, bf16[1,128,2048]{2,1,0:T(8,128)(2,1)S(1)} %get-tuple-element.14.c, ...), custom_call_target="tpu_custom_call" | custom-call | tf_op jit(solution)/shard_map/pallas_call | solution.py:451

commit v4 on v3

--- a/solution.py
+++ b/solution.py
@@ -261,10 +261,14 @@
             device_id=sibling, device_id_type=MESH)
 
     def attend(g):
-        @pl.when((g == 3) & (core == 1))
+        @pl.when((g == 2) & (core == 1))
         def _():
             pl.semaphore_wait(barrier, N_DP - 1)
             gain_along(0)
+
+        @pl.when((g == 3) & (core == 1))
+        def _():
+            gain_plane(0)
 
         forward_all(g).wait_recv()
         pltpu.make_async_copy(outbox.at[g, me], inbox.at[g, me], self_sem.at[g]).wait()
@@ -360,10 +364,6 @@
             for h in range(GH):
                 cols = pl.ds(pl.multiple_of((g * GH + h) * HD, HD), HD)
                 ref[0, :, cols] = home[h * TOK : (h + 1) * TOK, t * HD : (t + 1) * HD]
-
-    @pl.when(core == 1)
-    def _():
-        gain_plane(0)
 
     unpack(0)
 

time: 60.6 us -> 60.7 us (level)
  no operation moved by 1% of the time
where the time goes in v4:
time: 60.7 us; the launch traced here: 60.5 us
  Pallas kernels  59.9 us (99%)
  between operations  0.64 us (1%)
    pallas_call x1, Pallas kernels, on_device(): pl.pallas_call(kernel, out_shape=(rows, rows, rows, jax.ShapeDtypeStruct(...  58.7 us

profile of v4, /device:TPU:1, one launch (start us, length us, event | category | flops | bytes accessed | tf_op | source)
XLA Modules:
  0.0 60.5 jit_solution(18170829743520857104)
XLA Ops:
  0.6 58.7 %shard_map.93 = (bf16[1,128,2048]{2,1,0:T(8,128)(2,1)S(1)}, bf16[1,128,2048]{2,1,0:T(8,128)(2,1)S(1)}, bf16[1,128,2048]{2,1,0:T(8,128)(2,1)S(1)}, f32[16,128]{1,0:T(8,128)S(1)}) custom-call(bf16[1,128,2048]{2,1,0:T(8,128)(2,1)} %q_hbm.1, bf16[1,128,2048]{2,1,0:T(8,128)(2,1)} %k_hbm.1, bf16[1,128,2048]{2,1,0:T(8,128)(2,1)} %v_hbm.1, ...), custom_call_target="tpu_custom_call" | custom-call | tf_op jit(solution)/shard_map/pallas_call | solution.py:419
  59.3 1.2 %shard_map.94 = (bf16[1,128,2048]{2,1,0:T(8,128)(2,1)}, bf16[1,128,2048]{2,1,0:T(8,128)(2,1)}, bf16[1,128,2048]{2,1,0:T(8,128)(2,1)}, f32[16,128]{1,0:T(8,128)}) custom-call(bf16[1,128,2048]{2,1,0:T(8,128)(2,1)S(1)} %get-tuple-element.12.a, bf16[1,128,2048]{2,1,0:T(8,128)(2,1)S(1)} %get-tuple-element.13.b, bf16[1,128,2048]{2,1,0:T(8,128)(2,1)S(1)} %get-tuple-element.14.c, ...), custom_call_target="tpu_custom_call" | custom-call | tf_op jit(solution)/shard_map/pallas_call | solution.py:451
